TPU v7x, 256 devices: a whole 4x4x8 slice. The times are simulated.
256 devices in a mesh: grp: 4 (over y), row: 16 (over z_lo, x), col: 4 (over z_hi, core).
Axes of the slice: x: 4, y: 4, z: 8 (z_hi: 2, z_lo: 4; z = z_hi * 4 + z_lo), core: 2. Of those that a mesh axis runs over, the one named last changes fastest.
Arguments:
- teacher_in: bfloat16 [2048, 12288], P(('grp', 'col'), 'row'), may hold values from -6 to 6
- weight: bfloat16 [12288, 12288], P('row', ('grp', 'col')), may hold values from -0.0546875 to 0.0546875
- student_in: bfloat16 [2048, 12288], P(('grp', 'col'), 'row'), may hold values from -6 to 6
- kept_blocks: int32 [48], replicated, may hold values from 0 to 95, as said below
Outputs:
- gram_tile: float32 [6144, 6144], P('row', ('grp', 'col'))
- cross_tile: float32 [6144, 12288], P('row', ('grp', 'col'))
Inputs may be any that keep to these rules, and one draw needn't show every extreme that they name: `kept_blocks`: distinct, in rising order; the first and the last block are always kept.
All inputs are finite; a program needn't handle non-finite values.
Results may differ from a plain program's by a relative error of at most 0.0029.
Values may be sent and summed in bfloat16 or wider, within the bound.
A program may use at most 64 MiB of HBM per device.

v0:
```python
import jax
import jax.numpy as jnp
from jax import lax
from jax.sharding import PartitionSpec as P

BLOCK = 128


def local(teacher_in, weight, student_in, kept_blocks):
    tokens_all = lax.all_gather(teacher_in, ("grp", "col"), axis=0, tiled=True)
    partial_out = jnp.dot(tokens_all, weight, preferred_element_type=jnp.float32)
    teacher_out = lax.psum(partial_out, "row").astype(jnp.bfloat16)
    wide_rows = lax.all_gather(student_in, "row", axis=1, tiled=True)
    offsets = jnp.arange(BLOCK, dtype=jnp.int32)
    columns = (kept_blocks[:, None] * BLOCK + offsets[None, :]).reshape(-1)
    kept_local = jnp.take(wide_rows, columns, axis=1)
    width_row = kept_local.shape[1] // lax.axis_size("row")
    own_cols = lax.dynamic_slice_in_dim(kept_local, lax.axis_index("row") * width_row, width_row, 1)
    row_side = lax.all_gather(own_cols, ("grp", "col"), axis=0, tiled=True)
    col_side = lax.all_to_all(kept_local, ("grp", "col"), split_axis=1, concat_axis=0, tiled=True)
    inv_count = 1.0 / row_side.shape[0]
    dims = (((0,), (0,)), ((), ()))
    gram_tile = (
        lax.dot_general(row_side, col_side, dims, preferred_element_type=jnp.float32) * inv_count
    )
    cross_tile = (
        lax.dot_general(row_side, teacher_out, dims, preferred_element_type=jnp.float32) * inv_count
    )
    return (gram_tile, cross_tile)


def solution(mesh):
    return jax.shard_map(
        local,
        mesh=mesh,
        in_specs=(
            P(("grp", "col"), "row"),
            P("row", ("grp", "col")),
            P(("grp", "col"), "row"),
            P(),
        ),
        out_specs=(P("row", ("grp", "col")), P("row", ("grp", "col"))),
        check_vma=False,
    )
```

profile of v0, /device:TPU:32, one launch (start us, length us, event | category | flops | bytes accessed | tf_op | source)
XLA Modules:
  0.0 366.2 jit_solution(14701284763304304290)
XLA Ops:
  7.2 0.0 copy-start
  7.2 0.0 all-gather.4.cloned.1.call-start
  7.2 1.8 copy.7
  9.1 0.0 all-gather.4.cloned.1.call-update
  9.1 0.0 all-gather.8.cloned.1.call-start
  9.1 0.7 all-gather.8.cloned.1.call-update
  9.8 0.7 broadcast_multiply_fusion
  10.5 0.1 add.83
  10.6 0.1 compare_and_fusion.1
  10.7 0.1 dynamic-slice
  10.8 0.1 iota_add_fusion
  10.9 0.1 add.84
  11.0 81.3 %all-gather.4.cloned.1.call-done = bf16[128,12288]{0,1:T(8,128)(2,1)} async-done(((bf16[128,768]{0,1:T(8,128)(2,1)}), bf16[128,12288]{0,1:T(8,128)(2,1)}) %all-gather.4.cloned.1.call-update) | async-done | bytes 3145744 | tf_op jit(solution)/shard_map/all_gather | solution.py:13
  92.3 18.7 %gather_fusion = bf16[6144,128]{1,0:T(8,128)(2,1)S(1)} fusion(bf16[128,12288]{0,1:T(8,128)(2,1)} %all-gather.4.cloned.1.call-done, s32[6144]{0:T(1024)S(1)} %broadcast_clamp_fusion), kind=kCustom, calls=%fused_computation | custom fusion | bytes 3170304 | tf_op jit(solution)/shard_map/jit(_take)/gather | solution.py:16
  111.0 1.6 copy.8
  112.6 2.8 broadcast_select_fusion
  115.4 8.6 %all-to-all-start = ((bf16[128,16,384]{2,0,1:T(8,128)(2,1)}), bf16[128,16,384]{2,0,1:T(8,128)(2,1)}, u32[]{:S(2)}, u32[]{:S(2)}) async-start(bf16[128,16,384]{2,0,1:T(8,128)(2,1)} %broadcast_select_fusion), calls=%async_computation | async-start | bytes 3145728 | tf_op jit(solution)/shard_map/all_to_all | solution.py:20
  124.0 0.0 all-gather.6.cloned.1.call-start
  124.1 0.8 dynamic-slice_select_fusion
  124.9 0.0 all-gather.6.cloned.1.call-update
  124.9 66.2 %all-gather.8.cloned.1.call-done = bf16[2048,768]{1,0:T(8,128)(2,1)} async-done(((bf16[128,768]{1,0:T(8,128)(2,1)}), bf16[2048,768]{1,0:T(8,128)(2,1)}) %all-gather.8.cloned.1.call-update) | async-done | bytes 3145744 | tf_op jit(solution)/shard_map/all_gather | solution.py:10
  191.0 0.0 copy-done
  191.0 7.2 %fusion.5 = f32[2048,768]{1,0:T(8,128)} fusion(bf16[2048,768]{1,0:T(8,128)(2,1)} %all-gather.8.cloned.1.call-done, bf16[768,768]{1,0:T(8,128)(2,1)S(1)} %copy-done), kind=kOutput, calls=%fused_computation.16 | convolution fusion | flops 2415919104 | bytes 10616832 | tf_op jit(solution)/shard_map/dot_general | solution.py:11
  198.2 153.8 %all-reduce.1 = bf16[2048,768]{1,0:T(8,128)(2,1)} all-reduce(f32[2048,768]{1,0:T(8,128)} %fusion.5), channel_id=1, replica_groups=mesh['grp'=4,'row'=16,'col'=4] {'row'}, use_global_device_ids=true, to_apply=%region_0.0 | all-reduce | flops 1572864 | bytes 9437184 | tf_op jit(solution)/shard_map/psum | solution.py:12
  352.0 0.0 all-gather.6.cloned.1.call-done
  352.0 0.0 all-to-all-done
  352.0 0.0 copy-start.1
  352.0 3.8 %convolution_multiply_fusion = f32[384,384]{1,0:T(8,128)} fusion(bf16[2048,384]{0,1:T(8,128)(2,1)} %all-gather.6.cloned.1.call-done, bf16[2048,384]{1,0:T(8,128)(2,1)} %bitcast.6), kind=kOutput, calls=%fused_computation.5 | convolution fusion | flops 604127232 | bytes 3735552 | tf_op jit(solution)/shard_map/dot_general | solution.py:24
  355.9 0.0 copy-done.1
  355.9 3.8 %fusion.2 = f32[384,768]{1,0:T(8,128)} fusion(bf16[2048,384]{0,1:T(8,128)(2,1)} %all-gather.6.cloned.1.call-done, bf16[2048,768]{1,0:T(8,128)(2,1)S(1)} %copy-done.1), kind=kOutput, calls=%fused_computation.4 | convolution fusion | flops 1208254464 | bytes 5898240 | tf_op jit(solution)/shard_map/dot_general | solution.py:27
  (5 shorter events, 0.1 us)
Async XLA Ops:
  7.2 183.9 %copy-start = (bf16[768,768]{1,0:T(8,128)(2,1)S(1)}, bf16[768,768]{1,0:T(8,128)(2,1)}, u32[]{:S(2)}) copy-start(bf16[768,768]{1,0:T(8,128)(2,1)} %param.5) | copy-start | bytes 3538948
  7.2 85.1 %all-gather.4.cloned.1.call-start = ((), (), s32[]{:S(2)}) async-start(), calls=%async_computation.1 | async-start | bytes 3342336 | tf_op jit(solution)/shard_map/all_gather | solution.py:13
  9.1 182.0 %all-gather.8.cloned.1.call-start = ((), (), s32[]{:S(2)}) async-start(), calls=%async_computation.3 | async-start | bytes 3342336 | tf_op jit(solution)/shard_map/all_gather | solution.py:10
  115.4 236.6 %all-to-all-start = ((bf16[128,16,384]{2,0,1:T(8,128)(2,1)}), bf16[128,16,384]{2,0,1:T(8,128)(2,1)}, u32[]{:S(2)}, u32[]{:S(2)}) async-start(bf16[128,16,384]{2,0,1:T(8,128)(2,1)} %broadcast_select_fusion), calls=%async_computation | async-start | bytes 3145728 | tf_op jit(solution)/shard_map/all_to_all | solution.py:20
  124.0 228.0 %all-gather.6.cloned.1.call-start = ((), (), s32[]{:S(2)}) async-start(), calls=%async_computation.2 | async-start | bytes 1671168 | tf_op jit(solution)/shard_map/all_gather | solution.py:19
  352.0 3.8 %copy-start.1 = (bf16[2048,768]{1,0:T(8,128)(2,1)S(1)}, bf16[2048,768]{1,0:T(8,128)(2,1)}, u32[]{:S(2)}) copy-start(bf16[2048,768]{1,0:T(8,128)(2,1)} %all-reduce.1) | copy-start | bytes 9437188
Sparse Core Ops, SparseCore 0:
  10.4 81.8 all-gather.3
  94.9 96.0 all-gather.7
  194.2 128.4 all-gather.5
where the time goes:
time: 372 us; the launch traced here: 366 us
  blocking collectives  154 us (41%)
  waiting for transfers between devices  148 us (40%)
  local copies, waits for them, and re-layouts  22.4 us (6%)
  matrix products  14.8 us (4%)
  between operations  13.8 us (4%)
  starting transfers between devices  8.74 us (2%)
  other arithmetic  4.47 us (1%)
    psum x1, blocking collectives, local(): teacher_out = lax.psum(partial_out, 'row').astype(jnp.bfloat16)  154 us
    all_gather x1, waiting for transfers between devices, local(): wide_rows = lax.all_gather(student_in, 'row', axis=1, tiled=True)  81.3 us
    all_gather x1, waiting for transfers between devices, local(): tokens_all = lax.all_gather(teacher_in, ('grp', 'col'), axis=0, tiled=True)  66.2 us
    gather x2, local copies, waits for them, and re-layouts, local(): kept_local = jnp.take(wide_rows, columns, axis=1)  20.3 us
    all_to_all x1, starting transfers between devices, local(): lax.all_to_all(kept_local, ('grp', 'col'), split_axis=1, concat_axis=0, t...  8.62 us
  transfers between devices with their start and end apart: 4, of which 2 were waited for; matrix products, arithmetic and copies ran while one was open for 9% of the time, Pallas kernels for 0%

commit v1 on v0

v1 whole, which is shorter than its diff:
```python
import jax
import jax.numpy as jnp
from jax import lax
from jax.experimental import pallas as pl
from jax.experimental.pallas import tpu as pltpu
from jax.sharding import PartitionSpec as P

MESH = pl.DeviceIdType.MESH
F32 = jnp.float32
BF16 = jnp.bfloat16
RING = 4
TOK = 128
PIECE = TOK // RING
FEAT = 768
KEPT = 384
BLOCK = 128
SLOTS = KEPT // BLOCK
ZBLOCKS = RING * FEAT // BLOCK
ORDER = (0, 1, 3, 2)
INV = 1.0 / 2048
COPIES = 120


def wrap(v):
    return lax.rem(v + RING, RING)


def kernel(kept, x_ref, w_ref, s_ref, gram_ref, cross_ref,
           xg, part, xin, total, zin, tg, sg, pack, kin, tile, kr, kc,
           send_sem, recv_sem):
    y, row, col = lax.axis_index("grp"), lax.axis_index("row"), lax.axis_index("col")
    zl, x = lax.div(row, RING), lax.rem(row, RING)
    core = lax.rem(col, 2)
    sib = col + 1 - 2 * core
    far = wrap(col + 2)
    far_sib = wrap(sib + 2)

    def to_x(k):
        return (y, zl * RING + wrap(x + k), col)

    def to_y(k):
        return (wrap(y + k), row, col)

    def to_z(k):
        return (y, wrap(zl + k) * RING + x, col)

    to_far = (y, row, far)
    to_sib = (y, row, sib)
    flip = (zl, y * RING + col, x)
    off_diagonal = row != y * RING + col

    count = [0]
    sent = []

    def copy(src, dst, device):
        i = count[0]
        count[0] += 1
        return pltpu.make_async_remote_copy(
            src_ref=src, dst_ref=dst, send_sem=send_sem.at[i], recv_sem=recv_sem.at[i],
            device_id=device, device_id_type=MESH)

    def push(src, dst, device):
        c = copy(src, dst, device)
        c.start()
        sent.append(c)
        return c

    kin[...] = jnp.zeros_like(kin)
    barrier = pltpu.get_barrier_semaphore()
    peers = [to_far, to_sib] + [f(k) for f in (to_x, to_y, to_z) for k in (1, 2, 3)]
    for p in peers:
        pl.semaphore_signal(barrier, inc=1, device_id=p, device_id_type=MESH)

    @pl.when(off_diagonal)
    def _():
        pl.semaphore_signal(barrier, inc=1, device_id=flip, device_id_type=MESH)

    pl.semaphore_wait(barrier, len(peers) + off_diagonal.astype(jnp.int32))

    class Gather:
        def __init__(self, buf, own):
            self.buf = buf
            self.far = push(own, buf.at[y, col], to_far)
            self.sib = {(0, 0): push(own, buf.at[y, col], to_sib)}
            self.near = {(k, 0): push(own, buf.at[y, col], to_y(k)) for k in ORDER[1:]}
            buf[y, col] = own[...]

        def spread(self):
            self.far.wait_recv()
            piece = self.buf.at[y, far]
            self.sib[0, 1] = push(piece, piece, to_sib)
            for k in ORDER[1:]:
                self.near[k, 1] = push(piece, piece, to_y(k))

        def hand(self, k):
            for w, c in ((0, col), (1, far)):
                self.near[k, w].wait_recv()
                piece = self.buf.at[wrap(y - k), c]
                self.sib[k, w] = push(piece, piece, to_sib)

        def ready(self, k):
            for w in (0, 1):
                self.sib[k, w].wait_recv()

    gx = Gather(xg, x_ref)

    for b in range(FEAT // BLOCK):
        sg[x * 6 + b] = s_ref[:, b * BLOCK:(b + 1) * BLOCK]
    own_blocks = sg.at[pl.ds(x * 6, 6)]
    student = [push(own_blocks, own_blocks, to_x(k)) for k in (1, 3, 2)]

    rsx, rsz, agz, agx, fwd = {}, {}, {}, {}, {}
    quarter = [wrap(y - k) for k in ORDER]

    def stage_a(i):
        q = quarter[i]

        def body(h, carry):
            lhs = xg[q, pl.ds(2 * h, 2)].reshape(2 * TOK, FEAT)
            out = jnp.dot(lhs, w_ref[...], preferred_element_type=F32)
            part[i, 2 * h] = out[:TOK].astype(BF16)
            part[i, 2 * h + 1] = out[TOK:].astype(BF16)

            @pl.when(x == 2 * h)
            def _():
                total[i] = out[:TOK]

            @pl.when(x == 2 * h + 1)
            def _():
                total[i] = out[TOK:]

            return carry

        lax.fori_loop(0, 2, body, 0)
        for n, k in enumerate((1, 3, 2)):
            rsx[i, n] = push(part.at[i, wrap(x + k)], xin.at[i, n], to_x(k))

    def stage_b(i):
        for n in range(3):
            rsx[i, n].wait_recv()
        total[i] = (total[i] + xin[i, 0].astype(F32)) + (xin[i, 1].astype(F32) + xin[i, 2].astype(F32))
        for n, k in enumerate((1, 2, 3)):
            rsz[i, n] = push(total.at[i, pl.ds(wrap(zl + k) * PIECE, PIECE)], zin.at[i, n], to_z(k))

    def stage_c(i):
        for n in range(3):
            rsz[i, n].wait_recv()
        mine = pl.ds(zl * PIECE, PIECE)
        tg[quarter[i], x, mine] = ((total[i, mine] + zin[i, 0]) + (zin[i, 1] + zin[i, 2])).astype(BF16)
        piece = tg.at[quarter[i], x, mine]
        for k in (1, 2, 3):
            agz[i, k] = push(piece, piece, to_z(k))

    def stage_d(i):
        for k in (1, 2, 3):
            agz[i, k].wait_recv()
        piece = tg.at[quarter[i], x]
        for k in (1, 3):
            agx[i, k] = push(piece, piece, to_x(k))

    def stage_e(i):
        for k, lo in ((1, 0), (3, TOK // 2)):
            agx[i, k].wait_recv()
            piece = tg.at[quarter[i], wrap(x - k), pl.ds(lo, TOK // 2)]
            fwd[i, k] = push(piece, piece, to_x(k))

    def stage_f(i):
        for k in (1, 3):
            fwd[i, k].wait_recv()
        q = quarter[i]
        lhs = kr[q].reshape(RING * TOK, KEPT)
        rhs = tg[q].reshape(RING * TOK, FEAT)
        out = lax.dot_general(lhs, rhs, (((0,), (0,)), ((), ())), preferred_element_type=F32)
        if i == 0:
            cross_ref[...] = out
        elif i < 3:
            cross_ref[...] += out
        else:
            cross_ref[...] = (cross_ref[...] + out) * INV

    gx.spread()

    for c in student:
        c.wait_recv()

    def linked(src, dst):
        gap = dst - src
        return (gap == 1) | (gap == -1) | ((src == 2) & (dst == 0)) | ((src == 1) & (dst == 3))

    packs = []
    for k in range(RING):
        zt = wrap(zl + k)
        for j in range(SLOTS):
            at = kept[(zt * RING + x) * SLOTS + j] - zl * ZBLOCKS
            at = jnp.minimum(jnp.maximum(at, 0), ZBLOCKS - 1)
            if k == 0:
                kin[zl * SLOTS + j] = sg[at]
            else:
                pack[(k - 1) * SLOTS + j] = sg[at]
        if k:
            c = copy(pack.at[pl.ds((k - 1) * SLOTS, SLOTS)], kin.at[pl.ds(zl * SLOTS, SLOTS)], to_z(k))
            packs.append((k, c))

            @pl.when(linked(zl, zt))
            def _():
                c.start()

    gx.ready(0)
    stage_a(0)

    for k, c in packs:
        @pl.when(linked(wrap(zl - k), zl))
        def _():
            c.wait_recv()

    for j in range(SLOTS):
        at = kept[row * SLOTS + j]
        tile[:, j * BLOCK:(j + 1) * BLOCK] = kin[lax.div(at, ZBLOCKS) * SLOTS + j]
    gk = Gather(kr, tile)
    share = copy(tile, kc.at[col, y], flip)

    @pl.when(off_diagonal)
    def _():
        share.start()

    @pl.when(jnp.logical_not(off_diagonal))
    def _():
        kc[x, zl] = tile[...]

    gx.hand(ORDER[1])
    gx.ready(ORDER[1])
    stage_a(1)
    gk.spread()
    stage_b(0)

    gx.hand(ORDER[2])
    gx.ready(ORDER[2])
    stage_a(2)

    @pl.when(off_diagonal)
    def _():
        share.wait_recv()

    own_share = kc.at[x, zl]
    colz = [push(own_share, own_share, to_z(k)) for k in (1, 2, 3)]

    stage_b(1)
    stage_c(0)

    gx.hand(ORDER[3])
    gx.ready(ORDER[3])
    stage_a(3)

    for k in ORDER[1:]:
        gk.hand(k)
    stage_b(2)
    stage_c(1)
    stage_d(0)
    for c in colz:
        c.wait_recv()
    colx = {k: push(kc.at[x], kc.at[x], to_x(k)) for k in (1, 3)}
    stage_b(3)
    stage_c(2)
    stage_d(1)
    stage_e(0)
    for k in ORDER:
        gk.ready(k)
    stage_c(3)
    stage_d(2)
    stage_e(1)
    colf = {}
    for k, lo in ((1, 0), (3, 2)):
        colx[k].wait_recv()
        piece = kc.at[wrap(x - k), pl.ds(lo, 2)]
        colf[k] = push(piece, piece, to_x(k))
    stage_f(0)
    stage_d(3)
    stage_e(2)
    stage_f(1)
    for k in (1, 3):
        colf[k].wait_recv()

    def gram_body(j, carry):
        lhs = kr[:, j].reshape(RING * TOK, KEPT)
        rhs = kc[j].reshape(RING * TOK, KEPT)
        gram_ref[...] += lax.dot_general(lhs, rhs, (((0,), (0,)), ((), ())), preferred_element_type=F32)
        return carry

    gram_ref[...] = jnp.zeros_like(gram_ref)
    lax.fori_loop(0, RING, gram_body, 0)
    gram_ref[...] = gram_ref[...] * INV
    stage_e(3)
    stage_f(2)
    stage_f(3)

    for c in sent:
        c.wait_send()
    for k, c in packs:
        @pl.when(linked(zl, wrap(zl + k)))
        def _():
            c.wait_send()

    @pl.when(off_diagonal)
    def _():
        share.wait_send()


def local(teacher_in, weight, student_in, kept_blocks):
    vmem = pl.BlockSpec(memory_space=pltpu.VMEM)
    return pl.pallas_call(
        kernel,
        out_shape=(jax.ShapeDtypeStruct((KEPT, KEPT), F32),
                   jax.ShapeDtypeStruct((KEPT, FEAT), F32)),
        in_specs=[pl.BlockSpec(memory_space=pltpu.SMEM), vmem, vmem, vmem],
        out_specs=(vmem, vmem),
        scratch_shapes=[
            pltpu.VMEM((RING, RING, TOK, FEAT), BF16),
            pltpu.VMEM((RING, RING, TOK, FEAT), BF16),
            pltpu.VMEM((RING, 3, TOK, FEAT), BF16),
            pltpu.VMEM((RING, TOK, FEAT), F32),
            pltpu.VMEM((RING, 3, PIECE, FEAT), F32),
            pltpu.VMEM((RING, RING, TOK, FEAT), BF16),
            pltpu.VMEM((ZBLOCKS, TOK, BLOCK), BF16),
            pltpu.VMEM((3 * SLOTS, TOK, BLOCK), BF16),
            pltpu.VMEM((RING * SLOTS, TOK, BLOCK), BF16),
            pltpu.VMEM((TOK, KEPT), BF16),
            pltpu.VMEM((RING, RING, TOK, KEPT), BF16),
            pltpu.VMEM((RING, RING, TOK, KEPT), BF16),
            pltpu.SemaphoreType.DMA((COPIES,)),
            pltpu.SemaphoreType.DMA((COPIES,)),
        ],
        compiler_params=pltpu.CompilerParams(
            collective_id=0, has_side_effects=True, vmem_limit_bytes=48 << 20),
        name="gram_cross",
    )(kept_blocks, teacher_in, weight, student_in)


def solution(mesh):
    return jax.shard_map(
        local,
        mesh=mesh,
        in_specs=(
            P(("grp", "col"), "row"),
            P("row", ("grp", "col")),
            P(("grp", "col"), "row"),
            P(),
        ),
        out_specs=(P("row", ("grp", "col")), P("row", ("grp", "col"))),
        check_vma=False,
    )
```

time: 372 us -> 132 us (0.35)
  the two profiles are of different devices: /device:TPU:32 before, /device:TPU:106 now
where the time goes in v1:
time: 132 us; the launch traced here: 131 us
  Pallas kernels  125 us (95%)
  local copies, waits for them, and re-layouts  5.6 us (4%)
    pallas_call x1, Pallas kernels, local(): pl.pallas_call(kernel, out_shape=(jax.ShapeDtypeStruct((KEPT, KEPT), F32)...  125 us
    unnamed x10, local copies, waits for them, and re-layouts  5.6 us

profile of v1, /device:TPU:106, one launch (start us, length us, event | category | flops | bytes accessed | tf_op | source)
XLA Modules:
  0.0 131.4 jit_solution(2473092771884741602)
XLA Ops:
  0.6 0.0 copy-start
  0.6 1.3 copy-done
  1.9 0.0 copy-start.1
  1.9 0.9 copy-done.1
  2.8 0.0 copy-start.2
  2.8 0.9 copy-done.2
  3.8 0.0 copy-start.3
  3.8 0.7 copy-done.3
  4.4 125.1 %gram_cross.1 = (f32[384,384]{1,0:T(8,128)S(1)}, f32[384,768]{1,0:T(8,128)S(1)}) custom-call(s32[48]{0:T(128)S(1)} %copy-done.3, bf16[128,768]{1,0:T(8,128)(2,1)S(1)} %copy-done.1, bf16[768,768]{1,0:T(8,128)(2,1)S(1)} %copy-done, bf16[128,768]{1,0:T(8,128)(2,1)S(1)} %copy-done.2), custom_call_target="tpu_custom_call" | custom-call | tf_op jit(solution)/shard_map/gram_cross/pallas_call | solution.py:310
  129.5 0.8 copy.8
  130.3 1.0 copy.9
Async XLA Ops:
  0.6 1.3 copy-start
  1.9 0.9 copy-start.1
  2.8 0.9 copy-start.2
  3.8 0.7 copy-start.3

commit v2 on v0

v2 whole, which is shorter than its diff:
```python
import jax
import jax.numpy as jnp
from jax import lax
from jax.experimental import pallas as pl
from jax.experimental.pallas import tpu as pltpu
from jax.sharding import PartitionSpec as P

MESH = pl.DeviceIdType.MESH
F32 = jnp.float32
BF16 = jnp.bfloat16
RING = 4
TOK = 128
PAIR = 2 * TOK
SUB = PAIR // RING
HALF = SUB // 2
FEAT = 768
KEPT = 384
BLOCK = 128
OWN = FEAT // BLOCK
SLOTS = KEPT // BLOCK
ORDER = (0, 1, 3, 2)
CHUNKS = tuple((k, w) for w in (0, 1) for k in ORDER)
INV = 1.0 / 2048
COPIES = 180


def wrap(v):
    return lax.rem(v + RING, RING)


def always(body):
    body()


def kernel(kept, x_hbm, w_hbm, s_hbm, gram_ref, cross_ref,
           xg, wv, sblk, part, mine, xin, total, zin, zhalf, tg,
           packx, sx, packz, kin, tile, kr, kc,
           load_sem, send_sem, recv_sem):
    y, row, col = lax.axis_index("grp"), lax.axis_index("row"), lax.axis_index("col")
    zl, x = lax.div(row, RING), lax.rem(row, RING)
    zh, core = lax.div(col, 2), lax.rem(col, 2)
    sib = col + 1 - 2 * core
    far = wrap(col + 2)
    inner = (zl == 1) | (zl == 2)
    outer = jnp.logical_not(inner)

    def to_x(k):
        return (y, zl * RING + wrap(x + k), col)

    def to_y(k):
        return (wrap(y + k), row, col)

    def at_z(z):
        return (y, z * RING + x, col)

    to_far = (y, row, far)
    to_sib = (y, row, sib)
    flip = (zl, y * RING + col, x)
    off_diagonal = row != y * RING + col

    count = [0, 0]
    open_sends = []

    def copy(src, dst, device, recv=None):
        i = count[0]
        count[0] += 1
        if recv is None:
            recv = count[1]
            count[1] += 1
        return pltpu.make_async_remote_copy(
            src_ref=src, dst_ref=dst, send_sem=send_sem.at[i], recv_sem=recv_sem.at[recv],
            device_id=device, device_id_type=MESH)

    def push(src, dst, device, recv=None):
        c = copy(src, dst, device, recv)
        c.start()
        open_sends.append((always, c))
        return c

    loads = [pltpu.make_async_copy(x_hbm, xg.at[y, col], load_sem.at[0])]
    for b in range(OWN):
        loads.append(pltpu.make_async_copy(
            s_hbm.at[:, pl.ds(b * BLOCK, BLOCK)], sblk.at[b], load_sem.at[1 + b]))
    loads.append(pltpu.make_async_copy(w_hbm, wv, load_sem.at[1 + OWN]))
    for c in loads:
        c.start()

    kin[...] = jnp.zeros_like(kin)
    barrier = pltpu.get_barrier_semaphore()
    peers = [to_far, to_sib]
    for k in (1, 2, 3):
        peers += [to_x(k), to_y(k), at_z(wrap(zl + k))]
    for p in peers:
        pl.semaphore_signal(barrier, inc=1, device_id=p, device_id_type=MESH)

    @pl.when(off_diagonal)
    def _():
        pl.semaphore_signal(barrier, inc=1, device_id=flip, device_id_type=MESH)

    pl.semaphore_wait(barrier, len(peers) + off_diagonal.astype(jnp.int32))

    class Gather:
        def __init__(self, buf, own):
            self.buf = buf
            slot = buf.at[y, col]
            self.far = push(own, slot, to_far)
            self.sib = {(0, 0): push(own, slot, to_sib)}
            self.near = {(k, 0): push(own, slot, to_y(k)) for k in ORDER[1:]}

        def spread(self):
            self.far.wait_recv()
            piece = self.buf.at[y, far]
            self.sib[0, 1] = push(piece, piece, to_sib)
            for k in ORDER[1:]:
                self.near[k, 1] = push(piece, piece, to_y(k))

        def hand(self, k, w):
            self.near[k, w].wait_recv()
            piece = self.buf.at[wrap(y - k), far if w else col]
            self.sib[k, w] = push(piece, piece, to_sib)

        def ready(self, k, w):
            self.sib[k, w].wait_recv()

    loads[0].wait()
    gx = Gather(xg, xg.at[y, col])

    for b in range(OWN):
        loads[1 + b].wait()
    student = []
    for k in (1, 3, 2, 0):
        xt = wrap(x + k)
        for j in range(SLOTS):
            pick = jnp.int32(0)
            for zt in range(RING):
                p = kept[(zt * RING + xt) * SLOTS + j] - row * OWN
                pick = jnp.where((p >= 0) & (p < OWN), p, pick)
            if k == 0:
                sx[x * SLOTS + j] = sblk[pick]
            else:
                packx[(k - 1) * SLOTS + j] = sblk[pick]
        if k:
            student.append(push(packx.at[pl.ds((k - 1) * SLOTS, SLOTS)],
                                sx.at[pl.ds(x * SLOTS, SLOTS)], to_x(k)))

    def linked(src, dst):
        gap = dst - src
        return (gap == 1) | (gap == -1) | ((src == 2) & (dst == 0)) | ((src == 1) & (dst == 3))

    packs = []

    def send_packs():
        for c in student:
            c.wait_recv()
        for k in range(RING):
            zt = wrap(zl + k)
            for j in range(SLOTS):
                p = kept[(zt * RING + x) * SLOTS + j]
                block = sx[lax.rem(lax.div(p, OWN), RING) * SLOTS + j]
                if k == 0:
                    kin[zl * SLOTS + j] = block
                else:
                    packz[(k - 1) * SLOTS + j] = block
            if k:
                c = copy(packz.at[pl.ds((k - 1) * SLOTS, SLOTS)],
                         kin.at[pl.ds(zl * SLOTS, SLOTS)], at_z(zt))
                packs.append((k, c))
                goes = pl.when(linked(zl, zt))
                goes(c.start)
                open_sends.append((goes, c))

    def make_tile():
        for k, c in packs:
            pl.when(linked(wrap(zl - k), zl))(c.wait_recv)
        for j in range(SLOTS):
            p = kept[row * SLOTS + j]
            tile[:, j * BLOCK:(j + 1) * BLOCK] = kin[lax.div(p, RING * OWN) * SLOTS + j]
        kr[y, col] = tile[...]

    rsx, rsz, mid, agz, agx, fwd = {}, {}, {}, {}, {}, {}
    place = [(wrap(y - k), lax.rem(zh + w, 2)) for k, w in CHUNKS]

    def stage_a(i):
        k, w = CHUNKS[i]
        gx.ready(k, w)
        q, h = place[i]
        lhs = xg[q, pl.ds(2 * h, 2)].reshape(PAIR, FEAT)
        out = jnp.dot(lhs, wv[...], preferred_element_type=F32)
        part[i] = out.astype(BF16)
        mine[...] = out
        for n, k in enumerate((1, 3, 2)):
            rsx[i, n] = push(part.at[i, pl.ds(wrap(x + k) * SUB, SUB)], xin.at[i, n], to_x(k))
        total[i] = mine[pl.ds(x * SUB, SUB)]

    def stage_b(i):
        for n in range(3):
            rsx[i, n].wait_recv()
        total[i] = (total[i] + xin[i, 0].astype(F32)) + (xin[i, 1].astype(F32) + xin[i, 2].astype(F32))
        c = copy(total.at[i], zin.at[i], at_z(jnp.where(zl < 2, 1, 2)))
        pl.when(outer)(c.start)
        open_sends.append((pl.when(outer), c))
        rsz[i] = c

    def stage_c(i):
        c = copy(total.at[i, pl.ds(lax.rem(zl, 2) * HALF, HALF)], zhalf.at[i], at_z(3 - zl))
        mid[i] = c
        open_sends.append((pl.when(inner), c))

        @pl.when(inner)
        def _():
            rsz[i].wait_recv()
            total[i] = total[i] + zin[i]
            c.start()

    def stage_d(i):
        h = lax.rem(zl + 1, 2)
        rows = pl.ds(h * HALF, HALF)
        q, g = place[i]
        piece = tg.at[q, g, x, rows]
        base = count[1]
        count[1] += 2
        cs = [copy(piece, piece, at_z(wrap(zl + k)), base + h) for k in (1, 2, 3)]
        agz[i] = base
        for c in cs:
            open_sends.append((pl.when(inner), c))

        @pl.when(inner)
        def _():
            mid[i].wait_recv()
            tg[q, g, x, rows] = (total[i, rows] + zhalf[i]).astype(BF16)
            for c in cs:
                c.start()

    def stage_e(i):
        q, g = place[i]
        for h in (0, 1):
            piece = tg.at[q, g, x, pl.ds(h * HALF, HALF)]
            c = pltpu.make_async_remote_copy(
                src_ref=piece, dst_ref=piece, send_sem=send_sem.at[0],
                recv_sem=recv_sem.at[agz[i] + h], device_id=to_sib, device_id_type=MESH)
            pl.when(zl != h + 1)(c.wait_recv)
        piece = tg.at[q, g, x]
        for k in (1, 3):
            agx[i, k] = push(piece, piece, to_x(k))

    def stage_f(i):
        q, g = place[i]
        for k, lo in ((1, 0), (3, HALF)):
            agx[i, k].wait_recv()
            piece = tg.at[q, g, wrap(x - k), pl.ds(lo, HALF)]
            fwd[i, k] = push(piece, piece, to_x(k))

    def stage_g(i):
        for k in (1, 3):
            fwd[i, k].wait_recv()
        q, g = place[i]
        lhs = kr[q, pl.ds(2 * g, 2)].reshape(PAIR, KEPT)
        rhs = tg[q, g].reshape(PAIR, FEAT)
        out = lax.dot_general(lhs, rhs, (((0,), (0,)), ((), ())), preferred_element_type=F32)
        if i == 0:
            cross_ref[...] = out
        elif i < len(CHUNKS) - 1:
            cross_ref[...] += out
        else:
            cross_ref[...] = (cross_ref[...] + out) * INV

    loads[1 + OWN].wait()
    stage_a(0)
    send_packs()
    gx.hand(*CHUNKS[1])
    gx.hand(*CHUNKS[2])
    stage_a(1)
    stage_b(0)
    make_tile()
    gk = Gather(kr, tile)
    share = copy(tile, kc.at[col, y], flip)
    pl.when(off_diagonal)(share.start)
    open_sends.append((pl.when(off_diagonal), share))

    @pl.when(jnp.logical_not(off_diagonal))
    def _():
        kc[x, zl] = tile[...]

    stage_a(2)
    gx.spread()
    gx.hand(*CHUNKS[3])
    stage_b(1)
    stage_c(0)
    stage_a(3)
    stage_b(2)
    stage_c(1)
    stage_d(0)
    stage_a(4)
    gk.spread()
    gx.hand(*CHUNKS[5])
    stage_b(3)
    stage_c(2)
    stage_d(1)
    stage_e(0)
    stage_a(5)
    pl.when(off_diagonal)(share.wait_recv)
    own_share = kc.at[x, zl]
    colz = [push(own_share, own_share, at_z(wrap(zl + k))) for k in (1, 2, 3)]
    gx.hand(*CHUNKS[6])
    stage_b(4)
    stage_c(3)
    stage_d(2)
    stage_e(1)
    stage_f(0)
    stage_a(6)
    gx.hand(*CHUNKS[7])
    for k in ORDER[1:]:
        gk.hand(k, 0)
    stage_b(5)
    stage_c(4)
    stage_d(3)
    stage_e(2)
    stage_f(1)
    stage_a(7)
    for k in ORDER[1:]:
        gk.hand(k, 1)
    stage_b(6)
    stage_c(5)
    stage_d(4)
    stage_e(3)
    stage_f(2)
    for c in colz:
        c.wait_recv()
    colx = {k: push(kc.at[x], kc.at[x], to_x(k)) for k in (1, 3)}
    for k, w in CHUNKS:
        gk.ready(k, w)
    stage_g(0)
    stage_b(7)
    stage_c(6)
    stage_d(5)
    stage_e(4)
    stage_f(3)
    stage_g(1)
    stage_c(7)
    stage_d(6)
    stage_e(5)
    stage_f(4)
    stage_g(2)
    colf = {}
    for k, lo in ((1, 0), (3, 2)):
        colx[k].wait_recv()
        piece = kc.at[wrap(x - k), pl.ds(lo, 2)]
        colf[k] = push(piece, piece, to_x(k))
    stage_d(7)
    stage_e(6)
    stage_f(5)
    stage_g(3)
    stage_e(7)
    stage_f(6)
    stage_g(4)
    for k in (1, 3):
        colf[k].wait_recv()

    def gram_body(j, carry):
        lhs = kr[:, j].reshape(RING * TOK, KEPT)
        rhs = kc[j].reshape(RING * TOK, KEPT)
        gram_ref[...] += lax.dot_general(lhs, rhs, (((0,), (0,)), ((), ())), preferred_element_type=F32)
        return carry

    gram_ref[...] = jnp.zeros_like(gram_ref)
    lax.fori_loop(0, RING, gram_body, 0)
    gram_ref[...] = gram_ref[...] * INV
    stage_f(7)
    stage_g(5)
    stage_g(6)
    stage_g(7)

    for when, c in open_sends:
        when(c.wait_send)


def local(teacher_in, weight, student_in, kept_blocks):
    vmem = pl.BlockSpec(memory_space=pltpu.VMEM)
    hbm = pl.BlockSpec(memory_space=pltpu.HBM)
    n = len(CHUNKS)
    return pl.pallas_call(
        kernel,
        out_shape=(jax.ShapeDtypeStruct((KEPT, KEPT), F32),
                   jax.ShapeDtypeStruct((KEPT, FEAT), F32)),
        in_specs=[pl.BlockSpec(memory_space=pltpu.SMEM), hbm, hbm, hbm],
        out_specs=(vmem, vmem),
        scratch_shapes=[
            pltpu.VMEM((RING, RING, TOK, FEAT), BF16),
            pltpu.VMEM((FEAT, FEAT), BF16),
            pltpu.VMEM((OWN, TOK, BLOCK), BF16),
            pltpu.VMEM((n, PAIR, FEAT), BF16),
            pltpu.VMEM((PAIR, FEAT), F32),
            pltpu.VMEM((n, 3, SUB, FEAT), BF16),
            pltpu.VMEM((n, SUB, FEAT), F32),
            pltpu.VMEM((n, SUB, FEAT), F32),
            pltpu.VMEM((n, HALF, FEAT), F32),
            pltpu.VMEM((RING, 2, RING, SUB, FEAT), BF16),
            pltpu.VMEM((3 * SLOTS, TOK, BLOCK), BF16),
            pltpu.VMEM((RING * SLOTS, TOK, BLOCK), BF16),
            pltpu.VMEM((3 * SLOTS, TOK, BLOCK), BF16),
            pltpu.VMEM((RING * SLOTS, TOK, BLOCK), BF16),
            pltpu.VMEM((TOK, KEPT), BF16),
            pltpu.VMEM((RING, RING, TOK, KEPT), BF16),
            pltpu.VMEM((RING, RING, TOK, KEPT), BF16),
            pltpu.SemaphoreType.DMA((2 + OWN,)),
            pltpu.SemaphoreType.DMA((COPIES,)),
            pltpu.SemaphoreType.DMA((COPIES,)),
        ],
        compiler_params=pltpu.CompilerParams(
            collective_id=0, has_side_effects=True, vmem_limit_bytes=48 << 20),
        name="gram_cross",
    )(kept_blocks, teacher_in, weight, student_in)


def solution(mesh):
    return jax.shard_map(
        local,
        mesh=mesh,
        in_specs=(
            P(("grp", "col"), "row"),
            P("row", ("grp", "col")),
            P(("grp", "col"), "row"),
            P(),
        ),
        out_specs=(P("row", ("grp", "col")), P("row", ("grp", "col"))),
        check_vma=False,
    )
```

time: 372 us -> 117 us (0.31)
  the two profiles are of different devices: /device:TPU:32 before, /device:TPU:24 now
where the time goes in v2:
time: 117 us
  Pallas kernels  111 us (95%)
  local copies, waits for them, and re-layouts  5.6 us (5%)
    pallas_call x1, Pallas kernels, local(): pl.pallas_call(kernel, out_shape=(jax.ShapeDtypeStruct((KEPT, KEPT), F32)...  111 us
    unnamed x10, local copies, waits for them, and re-layouts  5.6 us

profile of v2, /device:TPU:24, one launch (start us, length us, event | category | flops | bytes accessed | tf_op | source)
XLA Modules:
  0.0 117.2 jit_solution(3796653373186599102)
XLA Ops:
  0.6 0.0 copy-start
  0.6 1.3 %copy-done = bf16[768,768]{1,0:T(8,128)(2,1)S(1)} copy-done((bf16[768,768]{1,0:T(8,128)(2,1)S(1)}, bf16[768,768]{1,0:T(8,128)(2,1)}, u32[]{:S(2)}) %copy-start) | copy-done | bytes 1179672
  1.9 0.0 copy-start.1
  1.9 0.9 copy-done.1
  2.8 0.0 copy-start.2
  2.8 0.9 copy-done.2
  3.8 0.0 copy-start.3
  3.8 0.7 copy-done.3
  4.4 110.9 %gram_cross.1 = (f32[384,384]{1,0:T(8,128)S(1)}, f32[384,768]{1,0:T(8,128)S(1)}) custom-call(s32[48]{0:T(128)S(1)} %copy-done.3, bf16[128,768]{1,0:T(8,128)(2,1)S(1)} %copy-done.1, bf16[768,768]{1,0:T(8,128)(2,1)S(1)} %copy-done, bf16[128,768]{1,0:T(8,128)(2,1)S(1)} %copy-done.2), custom_call_target="tpu_custom_call" | custom-call | tf_op jit(solution)/shard_map/gram_cross/pallas_call | solution.py:381
  115.3 0.8 copy.8
  116.2 1.0 copy.9
Async XLA Ops:
  0.6 1.3 %copy-start = (bf16[768,768]{1,0:T(8,128)(2,1)S(1)}, bf16[768,768]{1,0:T(8,128)(2,1)}, u32[]{:S(2)}) copy-start(bf16[768,768]{1,0:T(8,128)(2,1)} %w_hbm.1) | copy-start | bytes 3538948
  1.9 0.9 copy-start.1
  2.8 0.9 copy-start.2
  3.8 0.7 copy-start.3

commit v3 on v2

--- a/solution.py
+++ b/solution.py
@@ -22,6 +22,7 @@
 CHUNKS = tuple((k, w) for w in (0, 1) for k in ORDER)
 INV = 1.0 / 2048
 COPIES = 180
+VMEM = 65273856
 
 
 def wrap(v):
@@ -60,6 +61,8 @@
 
     count = [0, 0]
     open_sends = []
+    owed = {}
+    done = []
 
     def copy(src, dst, device, recv=None):
         i = count[0]
@@ -75,7 +78,12 @@
         c = copy(src, dst, device, recv)
         c.start()
         open_sends.append((always, c))
+        owed[id(c)] = (always, c)
         return c
+
+    def got(c):
+        when, c = owed.pop(id(c))
+        when(c.wait_recv)
 
     loads = [pltpu.make_async_copy(x_hbm, xg.at[y, col], load_sem.at[0])]
     for b in range(OWN):
@@ -108,19 +116,19 @@
             self.near = {(k, 0): push(own, slot, to_y(k)) for k in ORDER[1:]}
 
         def spread(self):
-            self.far.wait_recv()
+            got(self.far)
             piece = self.buf.at[y, far]
             self.sib[0, 1] = push(piece, piece, to_sib)
             for k in ORDER[1:]:
                 self.near[k, 1] = push(piece, piece, to_y(k))
 
         def hand(self, k, w):
-            self.near[k, w].wait_recv()
+            got(self.near[k, w])
             piece = self.buf.at[wrap(y - k), far if w else col]
             self.sib[k, w] = push(piece, piece, to_sib)
 
         def ready(self, k, w):
-            self.sib[k, w].wait_recv()
+            got(self.sib[k, w])
 
     loads[0].wait()
     gx = Gather(xg, xg.at[y, col])
@@ -151,7 +159,7 @@
 
     def send_packs():
         for c in student:
-            c.wait_recv()
+            got(c)
         for k in range(RING):
             zt = wrap(zl + k)
             for j in range(SLOTS):
@@ -168,10 +176,11 @@
                 goes = pl.when(linked(zl, zt))
                 goes(c.start)
                 open_sends.append((goes, c))
+                owed[id(c)] = (pl.when(linked(wrap(zl - k), zl)), c)
 
     def make_tile():
         for k, c in packs:
-            pl.when(linked(wrap(zl - k), zl))(c.wait_recv)
+            got(c)
         for j in range(SLOTS):
             p = kept[row * SLOTS + j]
             tile[:, j * BLOCK:(j + 1) * BLOCK] = kin[lax.div(p, RING * OWN) * SLOTS + j]
@@ -194,21 +203,24 @@
 
     def stage_b(i):
         for n in range(3):
-            rsx[i, n].wait_recv()
+            got(rsx[i, n])
         total[i] = (total[i] + xin[i, 0].astype(F32)) + (xin[i, 1].astype(F32) + xin[i, 2].astype(F32))
         c = copy(total.at[i], zin.at[i], at_z(jnp.where(zl < 2, 1, 2)))
         pl.when(outer)(c.start)
         open_sends.append((pl.when(outer), c))
+        owed[id(c)] = (pl.when(inner), c)
         rsz[i] = c
 
     def stage_c(i):
         c = copy(total.at[i, pl.ds(lax.rem(zl, 2) * HALF, HALF)], zhalf.at[i], at_z(3 - zl))
         mid[i] = c
+        owed[id(c)] = (pl.when(inner), c)
         open_sends.append((pl.when(inner), c))
+
+        got(rsz[i])
 
         @pl.when(inner)
         def _():
-            rsz[i].wait_recv()
             total[i] = total[i] + zin[i]
             c.start()
 
@@ -220,25 +232,29 @@
         base = count[1]
         count[1] += 2
         cs = [copy(piece, piece, at_z(wrap(zl + k)), base + h) for k in (1, 2, 3)]
-        agz[i] = base
+        agz[i] = []
+        for n in (0, 1):
+            c = pltpu.make_async_remote_copy(
+                src_ref=tg.at[q, g, x, pl.ds(n * HALF, HALF)],
+                dst_ref=tg.at[q, g, x, pl.ds(n * HALF, HALF)], send_sem=send_sem.at[0],
+                recv_sem=recv_sem.at[base + n], device_id=to_sib, device_id_type=MESH)
+            owed[id(c)] = (pl.when(zl != n + 1), c)
+            agz[i].append(c)
         for c in cs:
             open_sends.append((pl.when(inner), c))
 
+        got(mid[i])
+
         @pl.when(inner)
         def _():
-            mid[i].wait_recv()
             tg[q, g, x, rows] = (total[i, rows] + zhalf[i]).astype(BF16)
             for c in cs:
                 c.start()
 
     def stage_e(i):
         q, g = place[i]
-        for h in (0, 1):
-            piece = tg.at[q, g, x, pl.ds(h * HALF, HALF)]
-            c = pltpu.make_async_remote_copy(
-                src_ref=piece, dst_ref=piece, send_sem=send_sem.at[0],
-                recv_sem=recv_sem.at[agz[i] + h], device_id=to_sib, device_id_type=MESH)
-            pl.when(zl != h + 1)(c.wait_recv)
+        for c in agz[i]:
+            got(c)
         piece = tg.at[q, g, x]
         for k in (1, 3):
             agx[i, k] = push(piece, piece, to_x(k))
@@ -246,130 +262,97 @@
     def stage_f(i):
         q, g = place[i]
         for k, lo in ((1, 0), (3, HALF)):
-            agx[i, k].wait_recv()
+            got(agx[i, k])
             piece = tg.at[q, g, wrap(x - k), pl.ds(lo, HALF)]
             fwd[i, k] = push(piece, piece, to_x(k))
 
     def stage_g(i):
         for k in (1, 3):
-            fwd[i, k].wait_recv()
+            got(fwd[i, k])
         q, g = place[i]
         lhs = kr[q, pl.ds(2 * g, 2)].reshape(PAIR, KEPT)
         rhs = tg[q, g].reshape(PAIR, FEAT)
         out = lax.dot_general(lhs, rhs, (((0,), (0,)), ((), ())), preferred_element_type=F32)
-        if i == 0:
+        done.append(i)
+        if len(done) == 1:
             cross_ref[...] = out
-        elif i < len(CHUNKS) - 1:
+        elif len(done) < len(CHUNKS):
             cross_ref[...] += out
         else:
             cross_ref[...] = (cross_ref[...] + out) * INV
 
-    loads[1 + OWN].wait()
-    stage_a(0)
-    send_packs()
-    gx.hand(*CHUNKS[1])
-    gx.hand(*CHUNKS[2])
-    stage_a(1)
-    stage_b(0)
-    make_tile()
-    gk = Gather(kr, tile)
-    share = copy(tile, kc.at[col, y], flip)
-    pl.when(off_diagonal)(share.start)
-    open_sends.append((pl.when(off_diagonal), share))
-
-    @pl.when(jnp.logical_not(off_diagonal))
-    def _():
-        kc[x, zl] = tile[...]
-
-    stage_a(2)
-    gx.spread()
-    gx.hand(*CHUNKS[3])
-    stage_b(1)
-    stage_c(0)
-    stage_a(3)
-    stage_b(2)
-    stage_c(1)
-    stage_d(0)
-    stage_a(4)
-    gk.spread()
-    gx.hand(*CHUNKS[5])
-    stage_b(3)
-    stage_c(2)
-    stage_d(1)
-    stage_e(0)
-    stage_a(5)
-    pl.when(off_diagonal)(share.wait_recv)
-    own_share = kc.at[x, zl]
-    colz = [push(own_share, own_share, at_z(wrap(zl + k))) for k in (1, 2, 3)]
-    gx.hand(*CHUNKS[6])
-    stage_b(4)
-    stage_c(3)
-    stage_d(2)
-    stage_e(1)
-    stage_f(0)
-    stage_a(6)
-    gx.hand(*CHUNKS[7])
-    for k in ORDER[1:]:
-        gk.hand(k, 0)
-    stage_b(5)
-    stage_c(4)
-    stage_d(3)
-    stage_e(2)
-    stage_f(1)
-    stage_a(7)
-    for k in ORDER[1:]:
-        gk.hand(k, 1)
-    stage_b(6)
-    stage_c(5)
-    stage_d(4)
-    stage_e(3)
-    stage_f(2)
-    for c in colz:
-        c.wait_recv()
-    colx = {k: push(kc.at[x], kc.at[x], to_x(k)) for k in (1, 3)}
-    for k, w in CHUNKS:
-        gk.ready(k, w)
-    stage_g(0)
-    stage_b(7)
-    stage_c(6)
-    stage_d(5)
-    stage_e(4)
-    stage_f(3)
-    stage_g(1)
-    stage_c(7)
-    stage_d(6)
-    stage_e(5)
-    stage_f(4)
-    stage_g(2)
-    colf = {}
-    for k, lo in ((1, 0), (3, 2)):
-        colx[k].wait_recv()
-        piece = kc.at[wrap(x - k), pl.ds(lo, 2)]
-        colf[k] = push(piece, piece, to_x(k))
-    stage_d(7)
-    stage_e(6)
-    stage_f(5)
-    stage_g(3)
-    stage_e(7)
-    stage_f(6)
-    stage_g(4)
-    for k in (1, 3):
-        colf[k].wait_recv()
-
-    def gram_body(j, carry):
-        lhs = kr[:, j].reshape(RING * TOK, KEPT)
-        rhs = kc[j].reshape(RING * TOK, KEPT)
-        gram_ref[...] += lax.dot_general(lhs, rhs, (((0,), (0,)), ((), ())), preferred_element_type=F32)
-        return carry
-
-    gram_ref[...] = jnp.zeros_like(gram_ref)
-    lax.fori_loop(0, RING, gram_body, 0)
-    gram_ref[...] = gram_ref[...] * INV
-    stage_f(7)
-    stage_g(5)
-    stage_g(6)
-    stage_g(7)
-
+    def tile_out():
+        make_tile()
+        gather["k"] = Gather(kr, tile)
+        c = copy(tile, kc.at[col, y], flip)
+        pl.when(off_diagonal)(c.start)
+        open_sends.append((pl.when(off_diagonal), c))
+        owed[id(c)] = (pl.when(off_diagonal), c)
+        share.append(c)
+
+        @pl.when(jnp.logical_not(off_diagonal))
+        def _():
+            kc[x, zl] = tile[...]
+
+    def hand(which, i):
+        gather[which].hand(*CHUNKS[i])
+
+    def spread(which):
+        gather[which].spread()
+
+    def share_z():
+        got(share[0])
+        piece = kc.at[x, zl]
+        colz.extend(push(piece, piece, at_z(wrap(zl + k))) for k in (1, 2, 3))
+
+    def share_x():
+        for c in colz:
+            got(c)
+        for k in (1, 3):
+            colx[k] = push(kc.at[x], kc.at[x], to_x(k))
+
+    def share_fwd():
+        for k, lo in ((1, 0), (3, 2)):
+            got(colx[k])
+            piece = kc.at[wrap(x - k), pl.ds(lo, 2)]
+            colf[k] = push(piece, piece, to_x(k))
+
+    def k_ready():
+        for k, w in CHUNKS:
+            gather["k"].ready(k, w)
+
+    def gram():
+        for k in (1, 3):
+            got(colf[k])
+
+        def gram_body(j, carry):
+            lhs = kr[:, j].reshape(RING * TOK, KEPT)
+            rhs = kc[j].reshape(RING * TOK, KEPT)
+            gram_ref[...] += lax.dot_general(lhs, rhs, (((0,), (0,)), ((), ())), preferred_element_type=F32)
+            return carry
+
+        gram_ref[...] = jnp.zeros_like(gram_ref)
+        lax.fori_loop(0, RING, gram_body, 0)
+        gram_ref[...] = gram_ref[...] * INV
+
+    gather, share, colz, colx, colf = {"x": gx}, [], [], {}, {}
+    A, B, C, D, E, F, G = stage_a, stage_b, stage_c, stage_d, stage_e, stage_f, stage_g
+    steps = (
+        (loads[1 + OWN].wait,), (A, 0), (hand, "x", 2), (send_packs,), (A, 2), (spread, "x"), (B, 0),
+        (A, 4), (hand, "x", 3), (tile_out,), (A, 3), (hand, "x", 5), (hand, "x", 1), (C, 0), (A, 5),
+        (B, 2), (hand, "x", 7), (B, 3), (D, 0), (A, 1), (hand, "x", 6), (B, 4), (C, 2), (hand, "k", 3),
+        (A, 6), (C, 3), (D, 2), (A, 7), (hand, "k", 1), (B, 5), (spread, "k"), (D, 3), (hand, "k", 6),
+        (share_z,), (E, 0), (E, 2), (B, 7), (hand, "k", 2), (C, 5), (B, 1), (C, 4), (B, 6), (E, 3),
+        (F, 0), (F, 2), (share_x,), (D, 5), (D, 4), (C, 1), (E, 5), (hand, "k", 7), (C, 7),
+        (hand, "k", 5), (E, 4), (k_ready,), (C, 6), (D, 1), (share_fwd,), (G, 2), (F, 5), (D, 6),
+        (D, 7), (E, 1), (E, 6), (G, 5), (E, 7), (F, 4), (G, 0), (F, 6), (F, 1), (gram,), (F, 7), (F, 3),
+        (G, 4), (G, 1), (G, 6), (G, 7), (G, 3),
+    )
+    for step, *args in steps:
+        step(*args)
+
+    for when, c in tuple(owed.values()):
+        when(c.wait_recv)
     for when, c in open_sends:
         when(c.wait_send)
 
@@ -407,7 +390,7 @@
             pltpu.SemaphoreType.DMA((COPIES,)),
         ],
         compiler_params=pltpu.CompilerParams(
-            collective_id=0, has_side_effects=True, vmem_limit_bytes=48 << 20),
+            collective_id=0, has_side_effects=True, vmem_limit_bytes=VMEM),
         name="gram_cross",
     )(kept_blocks, teacher_in, weight, student_in)
 

time: 117 us -> 107 us (0.915)
  the two profiles are of different devices: /device:TPU:24 before, /device:TPU:32 now
where the time goes in v3:
time: 107 us; the launch traced here: 105 us
  Pallas kernels  102 us (95%)
  local copies, waits for them, and re-layouts  3.03 us (3%)
    pallas_call x1, Pallas kernels, local(): pl.pallas_call(kernel, out_shape=(jax.ShapeDtypeStruct((KEPT, KEPT), F32)...  102 us
    unnamed x4, local copies, waits for them, and re-layouts  3.03 us

profile of v3, /device:TPU:32, one launch (start us, length us, event | category | flops | bytes accessed | tf_op | source)
XLA Modules:
  0.0 105.3 jit_solution(7984798038397238466)
XLA Ops:
  0.6 101.6 %gram_cross.1 = (f32[384,384]{1,0:T(8,128)}, f32[384,768]{1,0:T(8,128)}) custom-call(s32[48]{0:T(128)} %kept.1, bf16[128,768]{1,0:T(8,128)(2,1)} %x_hbm.1, bf16[768,768]{1,0:T(8,128)(2,1)} %w_hbm.1, bf16[128,768]{1,0:T(8,128)(2,1)} %s_hbm.1), custom_call_target="tpu_custom_call" | custom-call | tf_op jit(solution)/shard_map/gram_cross/pallas_call | solution.py:364
  102.2 0.0 copy-start
  102.2 2.0 %copy.8 = f32[384,384]{1,0:T(8,128)} copy(f32[384,384]{1,0:T(8,128)} %get-tuple-element.4) | data formatting | bytes 1179648
  104.2 0.0 copy-done
  104.2 1.0 copy.9
Async XLA Ops:
  102.2 2.0 %copy-start = (f32[384,768]{1,0:T(8,128)S(1)}, f32[384,768]{1,0:T(8,128)}, u32[]{:S(2)}) copy-start(f32[384,768]{1,0:T(8,128)} %get-tuple-element.5) | copy-start | bytes 3538948

commit v4 on v3

--- a/solution.py
+++ b/solution.py
@@ -21,7 +21,8 @@
 ORDER = (0, 1, 3, 2)
 CHUNKS = tuple((k, w) for w in (0, 1) for k in ORDER)
 INV = 1.0 / 2048
-COPIES = 180
+COPIES = 240
+RELAYED = (0, 0, 0, 0, 1, 1, 1, 1)
 VMEM = 65273856
 
 
@@ -34,7 +35,7 @@
 
 
 def kernel(kept, x_hbm, w_hbm, s_hbm, gram_ref, cross_ref,
-           xg, wv, sblk, part, mine, xin, total, zin, zhalf, tg,
+           xg, wv, sblk, part, mine, hopin, both, xin, total, zin, zhalf, tg,
            packx, sx, packz, kin, tile, kr, kc,
            load_sem, send_sem, recv_sem):
     y, row, col = lax.axis_index("grp"), lax.axis_index("row"), lax.axis_index("col")
@@ -186,7 +187,7 @@
             tile[:, j * BLOCK:(j + 1) * BLOCK] = kin[lax.div(p, RING * OWN) * SLOTS + j]
         kr[y, col] = tile[...]
 
-    rsx, rsz, mid, agz, agx, fwd = {}, {}, {}, {}, {}, {}
+    hop, rsx, rsz, mid, agz, agx, fwd = {}, {}, {}, {}, {}, {}, {}
     place = [(wrap(y - k), lax.rem(zh + w, 2)) for k, w in CHUNKS]
 
     def stage_a(i):
@@ -196,15 +197,33 @@
         lhs = xg[q, pl.ds(2 * h, 2)].reshape(PAIR, FEAT)
         out = jnp.dot(lhs, wv[...], preferred_element_type=F32)
         part[i] = out.astype(BF16)
-        mine[...] = out
-        for n, k in enumerate((1, 3, 2)):
-            rsx[i, n] = push(part.at[i, pl.ds(wrap(x + k) * SUB, SUB)], xin.at[i, n], to_x(k))
-        total[i] = mine[pl.ds(x * SUB, SUB)]
+        mine[i] = out
+        if not RELAYED[i]:
+            for n, k in enumerate((1, 3, 2)):
+                rsx[i, n, 0] = push(part.at[i, pl.ds(wrap(x + k) * SUB, SUB)], xin.at[i, n], to_x(k))
+            return
+        for n, k in enumerate((1, 3)):
+            hop[i, n] = push(part.at[i, pl.ds(wrap(x + 2) * SUB + n * HALF, HALF)], hopin.at[i, n], to_x(k))
+        for n, k in enumerate((1, 3)):
+            lo = (1 - n) * HALF
+            rsx[i, n, 0] = push(part.at[i, pl.ds(wrap(x + k) * SUB + lo, HALF)],
+                                xin.at[i, n, pl.ds(lo, HALF)], to_x(k))
+
+    def stage_h(i):
+        for n, k in enumerate((1, 3)):
+            got(hop[i, n])
+            rows = pl.ds(wrap(x + k) * SUB + n * HALF, HALF)
+            both[i, n] = (mine[i, rows] + hopin[i, n].astype(F32)).astype(BF16)
+            rsx[i, n, 1] = push(both.at[i, n], xin.at[i, n, pl.ds(n * HALF, HALF)], to_x(k))
 
     def stage_b(i):
-        for n in range(3):
-            got(rsx[i, n])
-        total[i] = (total[i] + xin[i, 0].astype(F32)) + (xin[i, 1].astype(F32) + xin[i, 2].astype(F32))
+        own = mine[i, pl.ds(x * SUB, SUB)]
+        for n in range(2 if RELAYED[i] else 3):
+            for m in range(2 if RELAYED[i] else 1):
+                got(rsx[i, n, m])
+        if not RELAYED[i]:
+            own = own + xin[i, 2].astype(F32)
+        total[i] = own + (xin[i, 0].astype(F32) + xin[i, 1].astype(F32))
         c = copy(total.at[i], zin.at[i], at_z(jnp.where(zl < 2, 1, 2)))
         pl.when(outer)(c.start)
         open_sends.append((pl.when(outer), c))
@@ -300,30 +319,38 @@
     def spread(which):
         gather[which].spread()
 
-    def share_z():
-        got(share[0])
-        piece = kc.at[x, zl]
-        colz.extend(push(piece, piece, at_z(wrap(zl + k))) for k in (1, 2, 3))
-
-    def share_x():
-        for c in colz:
-            got(c)
-        for k in (1, 3):
-            colx[k] = push(kc.at[x], kc.at[x], to_x(k))
-
-    def share_fwd():
-        for k, lo in ((1, 0), (3, 2)):
-            got(colx[k])
-            piece = kc.at[wrap(x - k), pl.ds(lo, 2)]
-            colf[k] = push(piece, piece, to_x(k))
+    def share_here():
+        if share:
+            got(share.pop())
+        return kc.at[x, zl]
+
+    def share_z(k):
+        piece = share_here()
+        colz[k] = push(piece, piece, at_z(wrap(zl + k)))
+
+    def share_x(k):
+        if k:
+            got(colz[k])
+            piece = kc.at[x, wrap(zl - k)]
+        else:
+            piece = share_here()
+        for d in (1, 3):
+            colx[k, d] = push(piece, piece, to_x(d))
+
+    def share_fwd(h):
+        for k, d in ((2 * h, 1), (2 * h + 1, 3)):
+            for e in (1, 3):
+                got(colx[k, e])
+            piece = kc.at[wrap(x - d), wrap(zl - k)]
+            colf.append(push(piece, piece, to_x(d)))
 
     def k_ready():
         for k, w in CHUNKS:
             gather["k"].ready(k, w)
 
     def gram():
-        for k in (1, 3):
-            got(colf[k])
+        for c in colf:
+            got(c)
 
         def gram_body(j, carry):
             lhs = kr[:, j].reshape(RING * TOK, KEPT)
@@ -335,18 +362,19 @@
         lax.fori_loop(0, RING, gram_body, 0)
         gram_ref[...] = gram_ref[...] * INV
 
-    gather, share, colz, colx, colf = {"x": gx}, [], [], {}, {}
-    A, B, C, D, E, F, G = stage_a, stage_b, stage_c, stage_d, stage_e, stage_f, stage_g
+    gather, share, colz, colx, colf = {"x": gx}, [], {}, {}, []
+    A, H, B, C, D, E, F, G = stage_a, stage_h, stage_b, stage_c, stage_d, stage_e, stage_f, stage_g
     steps = (
-        (loads[1 + OWN].wait,), (A, 0), (hand, "x", 2), (send_packs,), (A, 2), (spread, "x"), (B, 0),
-        (A, 4), (hand, "x", 3), (tile_out,), (A, 3), (hand, "x", 5), (hand, "x", 1), (C, 0), (A, 5),
-        (B, 2), (hand, "x", 7), (B, 3), (D, 0), (A, 1), (hand, "x", 6), (B, 4), (C, 2), (hand, "k", 3),
-        (A, 6), (C, 3), (D, 2), (A, 7), (hand, "k", 1), (B, 5), (spread, "k"), (D, 3), (hand, "k", 6),
-        (share_z,), (E, 0), (E, 2), (B, 7), (hand, "k", 2), (C, 5), (B, 1), (C, 4), (B, 6), (E, 3),
-        (F, 0), (F, 2), (share_x,), (D, 5), (D, 4), (C, 1), (E, 5), (hand, "k", 7), (C, 7),
-        (hand, "k", 5), (E, 4), (k_ready,), (C, 6), (D, 1), (share_fwd,), (G, 2), (F, 5), (D, 6),
-        (D, 7), (E, 1), (E, 6), (G, 5), (E, 7), (F, 4), (G, 0), (F, 6), (F, 1), (gram,), (F, 7), (F, 3),
-        (G, 4), (G, 1), (G, 6), (G, 7), (G, 3),
+        (loads[1 + OWN].wait,), (A, 0), (hand, "x", 1), (hand, "x", 2), (send_packs,), (A, 1),
+        (spread, "x"), (B, 0), (A, 2), (tile_out,), (hand, "x", 5), (hand, "x", 6), (B, 1), (A, 5),
+        (C, 0), (A, 4), (hand, "x", 7), (H, 5), (B, 2), (A, 7), (D, 0), (spread, "k"), (hand, "x", 3),
+        (hand, "k", 3), (H, 4), (hand, "k", 1), (B, 5), (C, 1), (H, 7), (A, 6), (A, 3), (hand, "k", 6),
+        (B, 4), (C, 2), (E, 0), (D, 1), (hand, "k", 7), (C, 5), (D, 2), (H, 6), (B, 7), (hand, "k", 5),
+        (E, 1), (share_z, 1), (C, 4), (share_x, 0), (F, 0), (share_z, 3), (share_z, 2), (B, 3), (F, 1),
+        (E, 2), (hand, "k", 2), (share_x, 1), (C, 7), (D, 4), (D, 5), (share_x, 3), (F, 2),
+        (share_fwd, 0), (B, 6), (share_x, 2), (D, 7), (E, 4), (C, 3), (E, 5), (C, 6), (k_ready,),
+        (share_fwd, 1), (E, 7), (D, 3), (F, 5), (D, 6), (F, 4), (E, 3), (G, 2), (E, 6), (G, 0), (G, 1),
+        (G, 5), (F, 3), (G, 4), (F, 7), (F, 6), (gram,), (G, 3), (G, 7), (G, 6),
     )
     for step, *args in steps:
         step(*args)
@@ -372,7 +400,9 @@
             pltpu.VMEM((FEAT, FEAT), BF16),
             pltpu.VMEM((OWN, TOK, BLOCK), BF16),
             pltpu.VMEM((n, PAIR, FEAT), BF16),
-            pltpu.VMEM((PAIR, FEAT), F32),
+            pltpu.VMEM((n, PAIR, FEAT), F32),
+            pltpu.VMEM((n, 2, HALF, FEAT), BF16),
+            pltpu.VMEM((n, 2, HALF, FEAT), BF16),
             pltpu.VMEM((n, 3, SUB, FEAT), BF16),
             pltpu.VMEM((n, SUB, FEAT), F32),
             pltpu.VMEM((n, SUB, FEAT), F32),

time: 107 us -> 105 us (0.981)
  Pallas kernels: 102 us -> 100 us
    pallas_call x1, Pallas kernels: 102 us -> 100 us  [local(): pl.pallas_call(kernel, out_shape=(jax.ShapeDtypeStruct((KEPT, KEPT), F32)...]
where the time goes in v4:
time: 105 us; the launch traced here: 104 us
  Pallas kernels  100 us (95%)
  local copies, waits for them, and re-layouts  3.03 us (3%)
    pallas_call x1, Pallas kernels, local(): pl.pallas_call(kernel, out_shape=(jax.ShapeDtypeStruct((KEPT, KEPT), F32)...  100 us
    unnamed x4, local copies, waits for them, and re-layouts  3.03 us

profile of v4, /device:TPU:32, one launch (start us, length us, event | category | flops | bytes accessed | tf_op | source)
XLA Modules:
  0.0 104.1 jit_solution(16312434764663086120)
XLA Ops:
  0.6 100.5 %gram_cross.1 = (f32[384,384]{1,0:T(8,128)}, f32[384,768]{1,0:T(8,128)}) custom-call(s32[48]{0:T(128)} %kept.1, bf16[128,768]{1,0:T(8,128)(2,1)} %x_hbm.1, bf16[768,768]{1,0:T(8,128)(2,1)} %w_hbm.1, bf16[128,768]{1,0:T(8,128)(2,1)} %s_hbm.1), custom_call_target="tpu_custom_call" | custom-call | tf_op jit(solution)/shard_map/gram_cross/pallas_call | solution.py:392
  101.1 0.0 copy-start
  101.1 2.0 %copy.8 = f32[384,384]{1,0:T(8,128)} copy(f32[384,384]{1,0:T(8,128)} %get-tuple-element.4) | data formatting | bytes 1179648
  103.1 0.0 copy-done
  103.1 1.0 copy.9
Async XLA Ops:
  101.1 2.0 %copy-start = (f32[384,768]{1,0:T(8,128)S(1)}, f32[384,768]{1,0:T(8,128)}, u32[]{:S(2)}) copy-start(f32[384,768]{1,0:T(8,128)} %get-tuple-element.5) | copy-start | bytes 3538948

commit v5 on v4

--- a/solution.py
+++ b/solution.py
@@ -199,7 +199,7 @@
         part[i] = out.astype(BF16)
         mine[i] = out
         if not RELAYED[i]:
-            for n, k in enumerate((1, 3, 2)):
+            for n, k in enumerate((2, 1, 3)):
                 rsx[i, n, 0] = push(part.at[i, pl.ds(wrap(x + k) * SUB, SUB)], xin.at[i, n], to_x(k))
             return
         for n, k in enumerate((1, 3)):

time: 105 us -> 105 us (level)
  no operation moved by 1% of the time
where the time goes in v5:
time: 105 us; the launch traced here: 103 us
  Pallas kernels  99.8 us (95%)
  local copies, waits for them, and re-layouts  3.03 us (3%)
    pallas_call x1, Pallas kernels, local(): pl.pallas_call(kernel, out_shape=(jax.ShapeDtypeStruct((KEPT, KEPT), F32)...  99.8 us
    unnamed x4, local copies, waits for them, and re-layouts  3.03 us

profile of v5, /device:TPU:32, one launch (start us, length us, event | category | flops | bytes accessed | tf_op | source)
XLA Modules:
  0.0 103.5 jit_solution(539318643313653657)
XLA Ops:
  0.6 99.8 %gram_cross.1 = (f32[384,384]{1,0:T(8,128)}, f32[384,768]{1,0:T(8,128)}) custom-call(s32[48]{0:T(128)} %kept.1, bf16[128,768]{1,0:T(8,128)(2,1)} %x_hbm.1, bf16[768,768]{1,0:T(8,128)(2,1)} %w_hbm.1, bf16[128,768]{1,0:T(8,128)(2,1)} %s_hbm.1), custom_call_target="tpu_custom_call" | custom-call | tf_op jit(solution)/shard_map/gram_cross/pallas_call | solution.py:392
  100.4 0.0 copy-start
  100.4 2.0 %copy.8 = f32[384,384]{1,0:T(8,128)} copy(f32[384,384]{1,0:T(8,128)} %get-tuple-element.4) | data formatting | bytes 1179648
  102.4 0.0 copy-done
  102.4 1.0 copy.9
Async XLA Ops:
  100.4 2.0 %copy-start = (f32[384,768]{1,0:T(8,128)S(1)}, f32[384,768]{1,0:T(8,128)}, u32[]{:S(2)}) copy-start(f32[384,768]{1,0:T(8,128)} %get-tuple-element.5) | copy-start | bytes 3538948

commit v6 on v5

--- a/solution.py
+++ b/solution.py
@@ -137,7 +137,7 @@
     for b in range(OWN):
         loads[1 + b].wait()
     student = []
-    for k in (1, 3, 2, 0):
+    for k in (2, 1, 3, 0):
         xt = wrap(x + k)
         for j in range(SLOTS):
             pick = jnp.int32(0)
@@ -250,7 +250,7 @@
         piece = tg.at[q, g, x, rows]
         base = count[1]
         count[1] += 2
-        cs = [copy(piece, piece, at_z(wrap(zl + k)), base + h) for k in (1, 2, 3)]
+        cs = [copy(piece, piece, at_z(wrap(zl + k)), base + h) for k in (2, 1, 3)]
         agz[i] = []
         for n in (0, 1):
             c = pltpu.make_async_remote_copy(

time: 105 us -> 105 us (level)
  no operation moved by 1% of the time
where the time goes in v6:
time: 105 us; the launch traced here: 104 us
  Pallas kernels  100 us (95%)
  local copies, waits for them, and re-layouts  3.03 us (3%)
    pallas_call x1, Pallas kernels, local(): pl.pallas_call(kernel, out_shape=(jax.ShapeDtypeStruct((KEPT, KEPT), F32)...  100 us
    unnamed x4, local copies, waits for them, and re-layouts  3.03 us

profile of v6, /device:TPU:32, one launch (start us, length us, event | category | flops | bytes accessed | tf_op | source)
XLA Modules:
  0.0 103.7 jit_solution(15774992991075450827)
XLA Ops:
  0.6 100.1 %gram_cross.1 = (f32[384,384]{1,0:T(8,128)}, f32[384,768]{1,0:T(8,128)}) custom-call(s32[48]{0:T(128)} %kept.1, bf16[128,768]{1,0:T(8,128)(2,1)} %x_hbm.1, bf16[768,768]{1,0:T(8,128)(2,1)} %w_hbm.1, bf16[128,768]{1,0:T(8,128)(2,1)} %s_hbm.1), custom_call_target="tpu_custom_call" | custom-call | tf_op jit(solution)/shard_map/gram_cross/pallas_call | solution.py:392
  100.7 0.0 copy-start
  100.7 2.0 %copy.8 = f32[384,384]{1,0:T(8,128)} copy(f32[384,384]{1,0:T(8,128)} %get-tuple-element.4) | data formatting | bytes 1179648
  102.7 0.0 copy-done
  102.7 1.0 copy.9
Async XLA Ops:
  100.7 2.0 %copy-start = (f32[384,768]{1,0:T(8,128)S(1)}, f32[384,768]{1,0:T(8,128)}, u32[]{:S(2)}) copy-start(f32[384,768]{1,0:T(8,128)} %get-tuple-element.5) | copy-start | bytes 3538948

commit v7 on v5

--- a/solution.py
+++ b/solution.py
@@ -86,6 +86,15 @@
         when, c = owed.pop(id(c))
         when(c.wait_recv)
 
+    barrier = pltpu.get_barrier_semaphore()
+    peers = [to_far, to_sib] + [f(k) for f in (to_x, to_y) for k in (1, 2, 3)]
+    for p in peers:
+        pl.semaphore_signal(barrier, inc=1, device_id=p, device_id_type=MESH)
+
+    @pl.when(off_diagonal)
+    def _():
+        pl.semaphore_signal(barrier, inc=1, device_id=flip, device_id_type=MESH)
+
     loads = [pltpu.make_async_copy(x_hbm, xg.at[y, col], load_sem.at[0])]
     for b in range(OWN):
         loads.append(pltpu.make_async_copy(
@@ -95,18 +104,9 @@
         c.start()
 
     kin[...] = jnp.zeros_like(kin)
-    barrier = pltpu.get_barrier_semaphore()
-    peers = [to_far, to_sib]
     for k in (1, 2, 3):
-        peers += [to_x(k), to_y(k), at_z(wrap(zl + k))]
-    for p in peers:
-        pl.semaphore_signal(barrier, inc=1, device_id=p, device_id_type=MESH)
-
-    @pl.when(off_diagonal)
-    def _():
-        pl.semaphore_signal(barrier, inc=1, device_id=flip, device_id_type=MESH)
-
-    pl.semaphore_wait(barrier, len(peers) + off_diagonal.astype(jnp.int32))
+        pl.semaphore_signal(barrier, inc=1, device_id=at_z(wrap(zl + k)), device_id_type=MESH)
+    pl.semaphore_wait(barrier, len(peers) + 3 + off_diagonal.astype(jnp.int32))
 
     class Gather:
         def __init__(self, buf, own):

time: 105 us -> 106 us (level); the launches traced: 103 us -> 106 us
  Pallas kernels: 99.8 us -> 102 us
    pallas_call x1, Pallas kernels: 99.8 us -> 102 us  [local(): pl.pallas_call(kernel, out_shape=(jax.ShapeDtypeStruct((KEPT, KEPT), F32)...]
where the time goes in v7:
time: 106 us
  Pallas kernels  102 us (96%)
  local copies, waits for them, and re-layouts  3.03 us (3%)
    pallas_call x1, Pallas kernels, local(): pl.pallas_call(kernel, out_shape=(jax.ShapeDtypeStruct((KEPT, KEPT), F32)...  102 us
    unnamed x4, local copies, waits for them, and re-layouts  3.03 us

profile of v7, /device:TPU:32, one launch (start us, length us, event | category | flops | bytes accessed | tf_op | source)
XLA Modules:
  0.0 105.6 jit_solution(9761356155343316273)
XLA Ops:
  0.6 101.9 %gram_cross.1 = (f32[384,384]{1,0:T(8,128)}, f32[384,768]{1,0:T(8,128)}) custom-call(s32[48]{0:T(128)} %kept.1, bf16[128,768]{1,0:T(8,128)(2,1)} %x_hbm.1, bf16[768,768]{1,0:T(8,128)(2,1)} %w_hbm.1, bf16[128,768]{1,0:T(8,128)(2,1)} %s_hbm.1), custom_call_target="tpu_custom_call" | custom-call | tf_op jit(solution)/shard_map/gram_cross/pallas_call | solution.py:392
  102.6 0.0 copy-start
  102.6 2.0 %copy.8 = f32[384,384]{1,0:T(8,128)} copy(f32[384,384]{1,0:T(8,128)} %get-tuple-element.4) | data formatting | bytes 1179648
  104.6 0.0 copy-done
  104.6 1.0 copy.9
Async XLA Ops:
  102.6 2.0 %copy-start = (f32[384,768]{1,0:T(8,128)S(1)}, f32[384,768]{1,0:T(8,128)}, u32[]{:S(2)}) copy-start(f32[384,768]{1,0:T(8,128)} %get-tuple-element.5) | copy-start | bytes 3538948
